TPU v7x, 32 devices: a whole 2x2x4 slice. The times are simulated.
32 devices in a mesh: atom: 16 (over z, y, core), aux: 2 (over x).
Axes of the slice: x: 2, y: 2, z: 4, core: 2. Of those that a mesh axis runs over, the one named last changes fastest.
Arguments:
- three: bfloat16 [32, 128, 128, 384], P('atom', 'aux'), may hold values from -0.5 to 0.5
- occupied: bfloat16 [4096, 384], P(('atom', 'aux')), may hold values from -0.3125 to 0.3125
- virtual: bfloat16 [4096, 384], P(('atom', 'aux')), may hold values from -0.3125 to 0.3125
- three_mask: int32 [32, 3], replicated, may hold values from 0 to 1, as said below
- occ_mask: int32 [32, 3], replicated, may hold values from 0 to 1, as said below
- vir_mask: int32 [32, 3], replicated, may hold values from 0 to 1, as said below
- atom_sizes: int32 [32], replicated, may hold values from 64 to 128
Outputs:
- polarizability: float32 [32, 128, 384], P('atom', 'aux')
Inputs may be any that keep to these rules, and one draw needn't show every extreme that they name: three_mask[b, 1] = 1 for every block b; the slab pairs its atom blocks into molecules of two, and every block keeps its tile towards the neighbouring molecule: three_mask[b, 0] = 1 for even b and three_mask[b, 2] = 1 for odd b. occ_mask[b, 1] = 1 for every block b; occ_mask[b, 0] = 1 where b is a multiple of 2, and occ_mask[b, 2] = 1 where b + 1 is a multiple of 2. vir_mask[b, 1] = 1 for every block b.
All inputs are finite; a program needn't handle non-finite values.
Results may differ from a plain program's by a relative error of at most 0.0041.
Values may be sent and summed in bfloat16 or wider, within the bound.
A program may use at most 320 MiB of HBM per device.

v0:
```python
import jax
import jax.numpy as jnp
from jax import lax
from jax.sharding import PartitionSpec as P


def with_halo(cells, sides, width):
    for axis, dim in sides:
        count = lax.axis_size(axis)
        head = lax.slice_in_dim(cells, 0, width, axis=dim)
        tail = lax.slice_in_dim(cells, cells.shape[dim] - width, cells.shape[dim], axis=dim)
        cells = jnp.concatenate(
            [
                lax.ppermute(tail, axis, [(i, (i + 1) % count) for i in range(count)]),
                cells,
                lax.ppermute(head, axis, [((i + 1) % count, i) for i in range(count)]),
            ],
            axis=dim,
        )
    return cells


def from_behind(value, axis, steps):
    count = lax.axis_size(axis)
    pairs = [(source, (source + steps) % count) for source in range(count)]
    return lax.ppermute(value, axis, pairs)


def pick_sizes(lookup, blocks):
    matches = blocks[:, None] == jnp.arange(lookup.shape[0], dtype=jnp.int32)[None, :]
    return jnp.sum(jnp.where(matches, lookup[None, :], 0), axis=1)


def pick_rows(lookup, blocks):
    matches = blocks[:, None] == jnp.arange(lookup.shape[0], dtype=jnp.int32)[None, :]
    return jnp.sum(jnp.where(matches[:, :, None], lookup[None, :, :], 0), axis=1)


def block_ids(first_block, block_count, total_blocks):
    return (first_block + jnp.arange(block_count, dtype=jnp.int32) + total_blocks) % total_blocks


def band_live(atom_sizes, mask_table, blocks, block_width):
    total_blocks = atom_sizes.shape[0]
    block_count = blocks.shape[0]
    inside = jnp.arange(block_width, dtype=jnp.int32)
    partners = (
        blocks[:, None] + jnp.arange(3, dtype=jnp.int32)[None, :] + total_blocks - 1
    ) % total_blocks
    own_size = pick_sizes(atom_sizes, blocks)
    partner_size = pick_sizes(atom_sizes, partners.reshape(-1)).reshape(block_count, 3)
    live_blocks = pick_rows(mask_table, blocks) > 0
    row_ok = inside[None, :] < own_size[:, None]
    col_ok = inside[None, None, :] < partner_size[:, :, None]
    both = row_ok[:, :, None, None] & col_ok[:, None, :, :] & live_blocks[:, None, :, None]
    return both.reshape(block_count, block_width, 3 * block_width)


def block_live(mask_table, blocks, block_width):
    block_count = blocks.shape[0]
    live_blocks = pick_rows(mask_table, blocks) > 0
    spread = jnp.broadcast_to(
        live_blocks[:, None, :, None], (block_count, block_width, 3, block_width)
    )
    return spread.reshape(block_count * block_width, 3 * block_width)


def shards(three, occupied, virtual, three_mask, occ_mask, vir_mask, atom_sizes):
    zero_bf = jnp.zeros((), jnp.bfloat16)
    block_count = three.shape[0]
    aux_local = three.shape[1]
    block_width = three.shape[2]
    total_blocks = atom_sizes.shape[0]
    first_block = lax.axis_index("atom") * block_count
    local_ids = block_ids(first_block, block_count, total_blocks)
    band_ok = band_live(atom_sizes, three_mask, local_ids, block_width)
    coupling = jnp.where(band_ok[:, None], three, zero_bf)
    occ_rows, vir_rows = (
        lax.all_gather(occupied, "aux", axis=0, tiled=True),
        lax.all_gather(virtual, "aux", axis=0, tiled=True),
    )
    occ_live = jnp.where(block_live(occ_mask, local_ids, block_width), occ_rows, zero_bf)
    vir_live = jnp.where(block_live(vir_mask, local_ids, block_width), vir_rows, zero_bf)
    vir_ext = with_halo(vir_live, (("atom", 0),), block_width)
    mixed = None
    for offset in range(3):
        coupled = coupling[:, :, :, offset * block_width : (offset + 1) * block_width]
        partner_rows = vir_ext[offset * block_width : (offset + block_count) * block_width]
        partner_rows = partner_rows.reshape(block_count, block_width, 3 * block_width)
        product = jnp.einsum(
            "lpmb,lbc->lpmc", coupled, partner_rows, preferred_element_type=jnp.float32
        )
        padded = jnp.pad(
            product, ((0, 0), (0, 0), (0, 0), (offset * block_width, (2 - offset) * block_width))
        )
        mixed = padded if offset == 0 else mixed + padded
    mixed = mixed.astype(jnp.bfloat16)
    occ_tiles = occ_live.reshape(block_count, block_width, 3 * block_width)
    paired = []
    for target in range(3):
        density = occ_tiles[:, :, target * block_width : (target + 1) * block_width]
        screened = jnp.einsum(
            "lmj,lpmc->lpjc",
            density,
            mixed[:, :, :, target * block_width : (target + 3) * block_width],
            preferred_element_type=jnp.float32,
        )
        paired.append(screened.astype(jnp.bfloat16))
    from_left = from_behind(paired[2][-1], "atom", 1)
    from_right = from_behind(paired[0][0], "atom", -1)
    before = jnp.concatenate([from_left[None], paired[2][:-1]], axis=0)
    after = jnp.concatenate([paired[0][1:], from_right[None]], axis=0)
    sources = jnp.stack([before, paired[1], after], axis=1)
    total_aux = aux_local * lax.axis_size("aux")
    tile_sum = jnp.einsum(
        "lqrc,loprc->lqop",
        lax.all_gather(coupling, "aux", axis=1, tiled=True),
        sources,
        preferred_element_type=jnp.float32,
    )
    swapped = lax.all_to_all(tile_sum, "aux", split_axis=1, concat_axis=3, tiled=True)
    return swapped.reshape(block_count, aux_local, 3 * total_aux)


def solution(mesh):
    in_specs = (
        P("atom", "aux", None, None),
        P(("atom", "aux"), None),
        P(("atom", "aux"), None),
        P(),
        P(),
        P(),
        P(),
    )
    out_specs = P("atom", "aux", None)
    return jax.shard_map(shards, mesh=mesh, in_specs=in_specs, out_specs=out_specs, check_vma=False)
```

profile of v0, /device:TPU:6, one launch (start us, length us, event | category | flops | bytes accessed | tf_op | source)
XLA Modules:
  0.0 393.0 jit_solution(6158620312043457783)
XLA Ops:
  6.5 0.1 iota_compare_fusion.1
  6.6 0.1 add_add_fusion
  6.7 1.0 select_reduce_fusion.1
  7.7 0.1 copy.46
  7.8 0.1 broadcast_bitcast_fusion.1
  7.9 0.1 sub.11
  8.0 0.8 select_reduce_fusion.4
  8.8 0.8 select_reduce_fusion
  9.6 0.1 lt.62
  9.7 0.1 broadcast_bitcast_fusion
  9.8 0.1 iota_compare_fusion.2
  9.9 0.1 and_and_fusion
  10.0 10.5 %broadcast_select_fusion = bf16[2,64,128,384]{3,2,1,0:T(8,128)(2,1)} fusion(bf16[2,64,128,384]{3,2,1,0:T(8,128)(2,1)} %param.7, pred[2,128,384]{2,1,0:T(8,128)(4,1)S(1)} %and_and_fusion), kind=kLoop, calls=%fused_computation.15 | loop fusion | flops 6291456 | bytes 25264128 | tf_op jit(solution)/shard_map/jit(_where)/select_n | solution.py:77
  20.6 0.1 copy.47
  20.7 0.7 copy-done.1
  21.5 5.3 %all_gather.10 = bf16[256,384]{1,0:T(8,128)(2,1)S(1)} all-gather(bf16[128,384]{1,0:T(8,128)(2,1)S(1)} %copy-done.1), channel_id=1, replica_groups=mesh['atom'=16,'aux'=2] {'aux'}, dimensions={0}, use_global_device_ids=true | all-gather | bytes 294912 | tf_op jit(solution)/shard_map/all_gather | solution.py:80
  26.7 0.1 broadcast_in_dim.132
  26.9 0.1 bitcast_select_fusion.1
  27.1 1.7 collective-permute-start.1
  28.8 0.1 copy.48
  28.9 5.3 %all_gather.11 = bf16[256,384]{1,0:T(8,128)(2,1)S(1)} all-gather(bf16[128,384]{1,0:T(8,128)(2,1)S(1)} %copy-done.2), channel_id=1, replica_groups=mesh['atom'=16,'aux'=2] {'aux'}, dimensions={0}, use_global_device_ids=true | all-gather | bytes 294912 | tf_op jit(solution)/shard_map/all_gather | solution.py:79
  34.2 18.7 %fusion.16 = f32[2,64,128,384]{3,2,1,0:T(8,128)} fusion(bf16[2,128,384,1]{2,1,3,0:T(8,128)(2,1)S(1)} %bitcast.82, bf16[2,64,128,384]{3,2,1,0:T(8,128)(2,1)} %broadcast_select_fusion), kind=kOutput, calls=%fused_computation.20 | convolution fusion | flops 1610612736 | bytes 29556736 | tf_op jit(solution)/shard_map/lpmb,lbc->lpmc/dot_general | solution.py:90
  52.9 0.1 broadcast_in_dim.135
  53.0 0.1 bitcast_select_fusion
  53.2 15.1 %fusion.14 = f32[2,64,128,384]{3,2,1,0:T(8,128)} fusion(bf16[2,128,384,1]{2,1,3,0:T(8,128)(2,1)S(1)} %bitcast.89, bf16[2,64,128,384]{3,2,1,0:T(8,128)(2,1)} %broadcast_select_fusion), kind=kOutput, calls=%fused_computation.18 | convolution fusion | flops 1610612736 | bytes 29556736 | tf_op jit(solution)/shard_map/lpmb,lbc->lpmc/dot_general | solution.py:90
  68.3 13.9 %fusion.18 = f32[2,64,128,384]{3,2,1,0:T(8,128)} fusion(bf16[2,128,384,1]{2,1,3,0:T(8,128)(2,1)S(1)} %bitcast.88, bf16[2,64,128,384]{3,2,1,0:T(8,128)(2,1)} %broadcast_select_fusion), kind=kOutput, calls=%fused_computation.22 | convolution fusion | flops 1610612736 | bytes 29556736 | tf_op jit(solution)/shard_map/lpmb,lbc->lpmc/dot_general | solution.py:90
  82.2 31.3 %add_convert_fusion = bf16[2,64,128,640]{3,2,1,0:T(8,128)(2,1)} fusion(f32[2,64,128,384]{3,2,1,0:T(8,128)} %fusion.14, f32[2,64,128,384]{3,2,1,0:T(8,128)} %fusion.16, f32[2,64,128,384]{3,2,1,0:T(8,128)} %fusion.18), kind=kLoop, calls=%fused_computation | loop fusion | flops 31457280 | bytes 96468992 | tf_op jit(solution)/shard_map/convert_element_type | solution.py:97
  113.5 10.5 %convert_bitcast_fusion.2 = bf16[2,64,128,384]{2,3,1,0:T(8,128)(2,1)} fusion(bf16[2,64,128,640]{3,2,1,0:T(8,128)(2,1)} %add_convert_fusion, bf16[2,128,384]{2,1,0:T(8,128)(2,1)S(1)} %bitcast.85), kind=kOutput, calls=%fused_computation.14 | convolution fusion | flops 1616904192 | bytes 25231360 | tf_op jit(solution)/shard_map/lmj,lpmc->lpjc/dot_general | solution.py:102
  124.0 9.7 %slice_bitcast_fusion.1 = (bf16[64,128,384]{1,2,0:T(8,128)(2,1)}, bf16[1,64,128,384]{2,3,1,0:T(8,128)(2,1)S(1)}) fusion(bf16[2,64,128,384]{2,3,1,0:T(8,128)(2,1)} %convert_bitcast_fusion.2), kind=kLoop, calls=%fused_computation.17 | loop fusion | bytes 25165824 | tf_op jit(solution)/shard_map/squeeze | solution.py:109
  133.7 10.5 %convert_bitcast_fusion = bf16[2,64,128,384]{2,3,1,0:T(8,128)(2,1)} fusion(bf16[2,64,128,640]{3,2,1,0:T(8,128)(2,1)} %add_convert_fusion, bf16[2,128,384]{2,1,0:T(8,128)(2,1)S(1)} %bitcast.86), kind=kOutput, calls=%fused_computation.12 | convolution fusion | flops 1616904192 | bytes 25231360 | tf_op jit(solution)/shard_map/lmj,lpmc->lpjc/dot_general | solution.py:102
  144.2 12.5 %fusion.25 = (bf16[1,64,128,384]{2,3,1,0:T(8,128)(2,1)}, bf16[64,128,384]{1,2,0:T(8,128)(2,1)}) fusion(bf16[2,64,128,384]{2,3,1,0:T(8,128)(2,1)} %convert_bitcast_fusion), kind=kLoop, calls=%fused_computation.58 | loop fusion | bytes 25165824 | tf_op jit(solution)/shard_map/slice | solution.py:112
  156.7 1.7 collective-permute-start.3
  158.4 10.5 %convert_bitcast_fusion.1 = bf16[2,1,64,128,384]{3,4,2,0,1:T(8,128)(2,1)} fusion(bf16[2,64,128,640]{3,2,1,0:T(8,128)(2,1)} %add_convert_fusion, bf16[2,128,384]{2,1,0:T(8,128)(2,1)S(1)} %bitcast.87), kind=kOutput, calls=%fused_computation.13 | convolution fusion | flops 1616904192 | bytes 25231360 | tf_op jit(solution)/shard_map/lmj,lpmc->lpjc/dot_general | solution.py:102
  169.0 102.8 %collective-permute-done.2 = bf16[64,128,384]{1,2,0:T(8,128)(2,1)} collective-permute-done((bf16[64,128,384]{1,2,0:T(8,128)(2,1)}, bf16[64,128,384]{1,2,0:T(8,128)(2,1)}, u32[]{:S(2)}, u32[]{:S(2)}) %collective-permute-start.2) | collective-permute-done | bytes 6291488 | tf_op jit(solution)/shard_map/ppermute | solution.py:26
  271.8 9.2 %maximum_bitcast_fusion = bf16[2,1,64,128,384]{3,4,2,0,1:T(8,128)(2,1)} fusion(bf16[1,64,128,384]{2,3,1,0:T(8,128)(2,1)S(1)} %get-tuple-element.9, bf16[1,64,128,384]{2,3,1,0:T(8,128)(2,1)} %bitcast.16), kind=kLoop, calls=%fused_computation.10 | loop fusion | flops 6291456 | bytes 25165824 | tf_op jit(solution)/shard_map/stack | solution.py:113
  281.0 8.3 %maximum_bitcast_fusion.1 = bf16[2,1,64,128,384]{3,4,2,0,1:T(8,128)(2,1)} fusion(bf16[1,64,128,384]{2,3,1,0:T(8,128)(2,1)} %bitcast.26, bf16[1,64,128,384]{2,3,1,0:T(8,128)(2,1)S(1)} %copy-done), kind=kLoop, calls=%fused_computation.11 | loop fusion | flops 6291456 | bytes 25165824 | tf_op jit(solution)/shard_map/stack | solution.py:113
  289.3 25.7 %pad_maximum_fusion = bf16[2,3,64,128,384]{3,4,2,0,1:T(8,128)(2,1)} fusion(bf16[2,1,64,128,384]{3,4,2,0,1:T(8,128)(2,1)} %maximum_bitcast_fusion.1, bf16[2,1,64,128,384]{3,4,2,0,1:T(8,128)(2,1)} %convert_bitcast_fusion.1, bf16[2,1,64,128,384]{3,4,2,0,1:T(8,128)(2,1)} %maximum_bitcast_fusion), kind=kLoop, calls=%fused_computation.1 | loop fusion | flops 37748736 | bytes 75497472 | tf_op jit(solution)/shard_map/stack | solution.py:113
  315.1 0.8 all-gather.2.cloned.1.call-done
  315.8 32.1 %copy.65 = bf16[2,128,128,384,1]{2,1,3,4,0:T(8,128)(2,1)} copy(bf16[2,128,128,384,1]{3,2,1,0,4:T(8,128)(2,1)} %bitcast.81) | data formatting | bytes 50331648 | tf_op jit(solution)/shard_map/all_gather | solution.py:117
  347.9 27.3 %fusion.20 = f32[2,128,3,64]{1,3,2,0:T(8,128)S(1)} fusion(bf16[2,128,128,384,1]{2,1,3,4,0:T(8,128)(2,1)} %copy.65, bf16[2,3,64,128,384]{3,4,2,0,1:T(8,128)(2,1)} %pad_maximum_fusion), kind=kOutput, calls=%fused_computation.24 | convolution fusion | flops 4831838208 | bytes 63111168 | tf_op jit(solution)/shard_map/lqrc,loprc->lqop/dot_general | solution.py:115
  375.3 0.3 copy.54
  375.5 0.4 reshape.145
  376.0 6.8 %all_to_all.15 = f32[2,1,24576]{2,1,0:T(1,128)S(1)} all-to-all(f32[2,1,24576]{2,1,0:T(1,128)S(1)} %reshape.145), channel_id=1, replica_groups=mesh['atom'=16,'aux'=2] {'aux'}, dimensions={0} | all-to-all | bytes 393216 | tf_op jit(solution)/shard_map/all_to_all | solution.py:121
  382.8 0.5 broadcast.157
  383.3 1.2 reduce
  384.5 0.4 reshape.146
  384.9 0.3 copy.55
  385.2 1.0 reshape.136
  (21 shorter events, 0.2 us)
Async XLA Ops:
  6.5 309.3 %all-gather.2.cloned.1.call-start = ((), (), s32[]{:S(2)}) async-start(), calls=%async_computation.1 | async-start | bytes 37748736 | tf_op jit(solution)/shard_map/all_gather | solution.py:117
  20.6 0.9 copy-start.1
  20.6 8.3 %copy-start.2 = (bf16[128,384]{1,0:T(8,128)(2,1)S(1)}, bf16[128,384]{1,0:T(8,128)(2,1)}, u32[]{:S(2)}) copy-start(bf16[128,384]{1,0:T(8,128)(2,1)} %param.8) | copy-start | bytes 294916
  27.0 26.1 %collective-permute-start = (bf16[128,384]{1,0:T(8,128)(2,1)S(1)}, bf16[128,384]{1,0:T(8,128)(2,1)S(1)}, u32[]{:S(2)}, u32[]{:S(2)}) collective-permute-start(bf16[128,384]{1,0:T(8,128)(2,1)S(1)} %get-tuple-element.14), channel_id=1, source_target_pairs={{0,2},{2,4},{4,6},{6,8},{8,10},{10,12},{12,14},{14,16},{16,18},{18... | collective-permute-start | bytes 294920 | tf_op jit(solution)/shard_map/ppermute | solution.py:14
  27.1 26.1 %collective-permute-start.1 = (bf16[128,384]{1,0:T(8,128)(2,1)S(1)}, bf16[128,384]{1,0:T(8,128)(2,1)S(1)}, u32[]{:S(2)}, u32[]{:S(2)}) collective-permute-start(bf16[128,384]{1,0:T(8,128)(2,1)S(1)} %get-tuple-element.15), channel_id=1, source_target_pairs={{2,0},{4,2},{6,4},{8,6},{10,8},{12,10},{14,12},{16,14},{18,16},{20... | collective-permute-start | bytes 294920 | tf_op jit(solution)/shard_map/ppermute | solution.py:16
  133.7 138.1 %collective-permute-start.2 = (bf16[64,128,384]{1,2,0:T(8,128)(2,1)}, bf16[64,128,384]{1,2,0:T(8,128)(2,1)}, u32[]{:S(2)}, u32[]{:S(2)}) collective-permute-start(bf16[64,128,384]{1,2,0:T(8,128)(2,1)} %get-tuple-element.8), channel_id=1, source_target_pairs={{0,2},{2,4},{4,6},{6,8},{8,10},{10,12},{12,14},{14,16},{16,18},{18... | collective-permute-start | bytes 18874376 | tf_op jit(solution)/shard_map/ppermute | solution.py:26
  156.7 124.3 %collective-permute-start.3 = (bf16[64,128,384]{1,2,0:T(8,128)(2,1)}, bf16[64,128,384]{1,2,0:T(8,128)(2,1)}, u32[]{:S(2)}, u32[]{:S(2)}) collective-permute-start(bf16[64,128,384]{1,2,0:T(8,128)(2,1)} %get-tuple-element.11), channel_id=1, source_target_pairs={{0,30},{2,0},{4,2},{6,4},{8,6},{10,8},{12,10},{14,12},{16,14},{18,... | collective-permute-start | bytes 18874376 | tf_op jit(solution)/shard_map/ppermute | solution.py:26
  271.8 9.2 %copy-start = (bf16[1,64,128,384]{2,3,1,0:T(8,128)(2,1)S(1)}, bf16[1,64,128,384]{2,3,1,0:T(8,128)(2,1)}, u32[]{:S(2)}) copy-start(bf16[1,64,128,384]{2,3,1,0:T(8,128)(2,1)} %get-tuple-element.10) | copy-start | bytes 18874372
Sparse Core Ops, SparseCore 0:
  20.7 295.0 all-gather.1
where the time goes:
time: 397 us; the launch traced here: 393 us
  matrix products  107 us (27%)
  waiting for transfers between devices  104 us (26%)
  other arithmetic  89.5 us (23%)
  local copies, waits for them, and re-layouts  58.8 us (15%)
  blocking collectives  17.4 us (4%)
  between operations  13.5 us (3%)
    ppermute x2, waiting for transfers between devices, from_behind(): return lax.ppermute(value, axis, pairs)  103 us
    dot_general x3, matrix products, shards(): jnp.einsum('lpmb,lbc->lpmc', coupled, partner_rows, preferred_element_typ...  47.7 us
    another operation x3, other arithmetic, shards(): sources = jnp.stack([before, paired[1], after], axis=1)  43.3 us
    all_gather x1, local copies, waits for them, and re-layouts, shards(): lax.all_gather(coupling, 'aux', axis=1, tiled=True)  32.1 us
    dot_general x3, matrix products, shards(): jnp.einsum('lmj,lpmc->lpjc', density, mixed[:, :, :, target * block_width...  31.6 us
    convert_element_type x1, other arithmetic, shards(): mixed = mixed.astype(jnp.bfloat16)  31.3 us
    dot_general x1, matrix products, shards(): jnp.einsum('lqrc,loprc->lqop', lax.all_gather(coupling, 'aux', axis=1, ti...  27.3 us
    slice x1, local copies, waits for them, and re-layouts, shards(): after = jnp.concatenate([paired[0][1:], from_right[None]], axis=0)  12.5 us
  transfers between devices with their start and end apart: 5, of which 2 were waited for; matrix products, arithmetic and copies ran while one was open for 45% of the time, Pallas kernels for 0%

commit v1 on v0

v1 whole, which is shorter than its diff:
```python
import jax
import jax.numpy as jnp
from jax import lax
from jax.sharding import PartitionSpec as P

CHUNKS = (16, 48, 48, 16)


def shift(value, axis, steps):
    count = lax.axis_size(axis)
    pairs = [(source, (source + steps) % count) for source in range(count)]
    return lax.ppermute(value, axis, pairs)


def shards(three, occupied, virtual, three_mask, occ_mask, vir_mask, atom_sizes):
    bf = jnp.bfloat16
    f32 = jnp.float32
    nb, aux_local, width, _ = three.shape
    total = atom_sizes.shape[0]
    first = lax.axis_index("atom") * nb
    side = lax.axis_index("aux")

    bounds = []
    low = 0
    for rows in CHUNKS:
        bounds.append((low, low + rows))
        low += rows
    local = [three[:, :, lo:hi].transpose(0, 2, 1, 3) for lo, hi in bounds]
    both = [lax.all_gather(piece, "aux", axis=0, tiled=False) for piece in local]

    vir_rows = lax.all_gather(virtual, "aux", axis=0, tiled=True)
    occ_rows = lax.all_gather(occupied, "aux", axis=0, tiled=True)
    vir_rows = vir_rows.reshape(nb, width, 3 * width)
    vir_ext = jnp.concatenate(
        [shift(vir_rows[-1:], "atom", 1), vir_rows, shift(vir_rows[:1], "atom", -1)], axis=0
    )

    ids = jnp.arange(total, dtype=jnp.int32)
    near = (ids[:, None] + jnp.arange(-1, 2, dtype=jnp.int32)[None, :] + total) % total
    inside = jnp.arange(width, dtype=jnp.int32)
    fits = inside[None, :] < atom_sizes[:, None]

    def window(table, start, length):
        rolled = jnp.roll(table, -(first + start), axis=0)
        return rolled[:length]

    fits_w = window(fits, -2, nb + 4)
    tm = window(three_mask > 0, -1, nb + 2)
    vm = window(vir_mask > 0, -1, nb + 2)
    om = window(occ_mask > 0, 0, nb)

    bands = []
    densities = []
    for l in range(nb):
        rows = []
        for o in range(3):
            b = l + o
            tile = vir_ext[b].reshape(width, 3, width)
            cols_ok = fits_w[b : b + 3]
            row_ok = fits_w[b + 1] & tm[l + 1, o]
            ok = row_ok[:, None, None] & (cols_ok & vm[b][:, None])[None]
            tile = jnp.where(ok, tile, 0).reshape(width, 3 * width)
            rows.append(jnp.pad(tile, ((0, 0), (o * width, (2 - o) * width))))
        bands.append(jnp.concatenate(rows, axis=0))
        occ = occ_rows[l * width : (l + 1) * width].reshape(width, 3, width)
        targets = fits_w[l + 1 : l + 4]
        ok = fits_w[l + 2][:, None, None] & (targets & om[l][:, None])[None]
        densities.append(jnp.where(ok, occ, 0))
    band = jnp.stack(bands).astype(bf)
    density = jnp.stack(densities).astype(bf)

    mixed = jnp.einsum("lpmb,lbk->lpmk", three, band, preferred_element_type=f32).astype(bf)
    keep = [tm[t : t + nb] for t in range(3)]

    def pair(t):
        out = jnp.einsum(
            "lmj,lpmc->ljpc",
            density[:, :, t],
            mixed[:, :, :, t * width : (t + 3) * width],
            preferred_element_type=f32,
        )
        ok = jnp.repeat(keep[t], width, axis=1)
        return jnp.where(ok[:, None, None, :], out, 0).astype(bf)

    up = pair(2)
    from_left = shift(up[-1:], "atom", 1)
    down = pair(0)
    from_right = shift(down[:1], "atom", -1)
    mid = pair(1)
    before = jnp.concatenate([from_left, up[:-1]], axis=0)
    after = jnp.concatenate([down[1:], from_right], axis=0)
    sources = jnp.stack([before, mid, after], axis=2)

    def contract(pieces):
        acc = None
        for (lo, hi), piece in zip(bounds, pieces):
            part = jnp.einsum(
                "lrqc,lropc->lqop", piece, sources[:, lo:hi], preferred_element_type=f32
            )
            acc = part if acc is None else acc + part
        return acc

    parts = [contract([piece[s] for piece in both]) for s in range(2)]
    own = jnp.where(side == 0, parts[0], parts[1])
    cross = jnp.where(side == 0, parts[1], parts[0])
    got = shift(cross, "aux", 1)
    sides = jnp.where(
        side == 0,
        jnp.concatenate([own, got], axis=3),
        jnp.concatenate([got, own], axis=3),
    )
    return sides.reshape(nb, aux_local, -1)


def solution(mesh):
    in_specs = (
        P("atom", "aux", None, None),
        P(("atom", "aux"), None),
        P(("atom", "aux"), None),
        P(),
        P(),
        P(),
        P(),
    )
    out_specs = P("atom", "aux", None)
    return jax.shard_map(shards, mesh=mesh, in_specs=in_specs, out_specs=out_specs, check_vma=False)
```

time: 397 us -> 388 us (0.977)
  other arithmetic: 89.5 us -> 59.8 us
  matrix products: 107 us -> 118 us
  waiting for transfers between devices: 104 us -> 111 us
  local copies, waits for them, and re-layouts: 58.8 us -> 64.6 us
    all_gather x1 -> x0, local copies, waits for them, and re-layouts: 32.1 us -> none  [shards(): lax.all_gather(coupling, 'aux', axis=1, tiled=True)]
    convert_element_type x1 -> x0, other arithmetic: 31.3 us -> none  [shards(): mixed = mixed.astype(jnp.bfloat16)]
    slice x2 -> x15, local copies, waits for them, and re-layouts: 12.5 us -> 43 us  [the longest x1 10.9 us: shards(): from_left = shift(up[-1:], 'atom', 1)]
    unnamed x11 -> x39, local copies, waits for them, and re-layouts: 1.69 us -> 21.3 us
    dot_general x7 -> x12, matrix products: 107 us -> 118 us  [the longest x8 62.4 us: contract(): jnp.einsum('lrqc,lropc->lqop', piece, sources[:, lo:hi], preferred_elemen...]
    squeeze x1 -> x0, local copies, waits for them, and re-layouts: 9.68 us -> none  [shards(): from_left = from_behind(paired[2][-1], 'atom', 1)]
    slice x0 -> x1, other arithmetic: none -> 9.38 us  [contract(): sources[:, lo:hi]]
    select_n x5 -> x6, other arithmetic: 10.7 us -> 1.52 us  [the longest x1 0.85 us: shards(): jnp.where(side == 0, jnp.concatenate([own, got], axis=3), jnp.concatenate...]
  transfers between devices with their start and end apart: 5 -> 9, of which waited for: 2 -> 2; matrix products, arithmetic and copies ran while one was open for 45% -> 57% of each run, Pallas kernels for 0% -> 0%
where the time goes in v1:
time: 388 us; the launch traced here: 387 us
  matrix products  118 us (30%)
  waiting for transfers between devices  111 us (29%)
  local copies, waits for them, and re-layouts  64.6 us (17%)
  other arithmetic  59.8 us (15%)
  blocking collectives  16 us (4%)
  between operations  13.6 us (4%)
  starting transfers between devices  4.23 us (1%)
    ppermute x5, waiting for transfers between devices, shift(): return lax.ppermute(value, axis, pairs)  111 us
    dot_general x8, matrix products, contract(): jnp.einsum('lrqc,lropc->lqop', piece, sources[:, lo:hi], preferred_elemen...  62.4 us
    another operation x3, other arithmetic, shards(): sources = jnp.stack([before, mid, after], axis=2)  44.6 us
    dot_general x3, matrix products, pair(): jnp.einsum('lmj,lpmc->ljpc', density[:, :, t], mixed[:, :, :, t * width:(...  28.4 us
    dot_general x1, matrix products, shards(): jnp.einsum('lpmb,lbk->lpmk', three, band, preferred_element_type=f32)  27.1 us
    unnamed x39, local copies, waits for them, and re-layouts  21.3 us
    slice x1, local copies, waits for them, and re-layouts, shards(): from_left = shift(up[-1:], 'atom', 1)  10.9 us
    slice x1, local copies, waits for them, and re-layouts, shards(): after = jnp.concatenate([down[1:], from_right], axis=0)  10.7 us
  transfers between devices with their start and end apart: 9, of which 2 were waited for; matrix products, arithmetic and copies ran while one was open for 57% of the time, Pallas kernels for 0%

profile of v1, /device:TPU:6, one launch (start us, length us, event | category | flops | bytes accessed | tf_op | source)
XLA Modules:
  0.0 387.1 jit_solution(6457968443646747329)
XLA Ops:
  6.5 2.2 fusion.106
  8.8 1.5 copy.160
  10.4 7.0 %fusion.107 = (bf16[2,64,48,384]{3,2,1,0:T(8,128)(2,1)S(1)}, bf16[2,64,48,384]{3,2,1,0:T(8,128)(2,1)}) fusion(bf16[2,64,128,384]{3,2,1,0:T(8,128)(2,1)} %param.9), kind=kLoop, calls=%fused_computation.153 | loop fusion | bytes 18874368 | tf_op jit(solution)/shard_map/slice | solution.py:28
  17.3 3.4 copy.159
  20.9 0.1 copy.54
  21.0 8.0 %all_gather.31 = bf16[256,384]{0,1:T(8,128)(2,1)S(1)} all-gather(bf16[128,384]{0,1:T(8,128)(2,1)S(1)} %copy.54), channel_id=1, replica_groups=mesh['atom'=16,'aux'=2] {'aux'}, dimensions={0}, use_global_device_ids=true | all-gather | bytes 294912 | tf_op jit(solution)/shard_map/all_gather | solution.py:31
  29.6 0.2 slice_reduce_fusion.5
  29.8 0.2 slice_reduce_fusion.3
  30.1 0.7 fusion.112
  30.7 2.5 broadcast_and_fusion.3
  33.3 0.2 and_select_fusion.4
  33.6 1.7 collective-permute-start.1
  35.3 5.7 %copy.158 = bf16[2,64,48,384]{3,1,2,0:T(8,128)(2,1)} copy(bf16[2,64,48,384]{3,2,1,0:T(8,128)(2,1)} %get-tuple-element.19) | data formatting | bytes 9437184
  41.2 8.0 %all_gather.30 = bf16[256,384]{1,0:T(8,128)(2,1)S(1)} all-gather(bf16[128,384]{1,0:T(8,128)(2,1)S(1)} %copy-done.2), channel_id=1, replica_groups=mesh['atom'=16,'aux'=2] {'aux'}, dimensions={0}, use_global_device_ids=true | all-gather | bytes 294912 | tf_op jit(solution)/shard_map/all_gather | solution.py:32
  49.3 0.1 copy.53
  49.4 0.1 copy.52
  49.5 0.1 copy.51
  49.8 1.3 slice_bitcast_fusion.47
  51.1 0.1 and_select_fusion.6
  51.2 0.1 and_select_fusion.7
  51.5 0.1 and_select_fusion.5
  51.7 0.1 and_select_fusion
  51.8 27.1 %convert_bitcast_fusion = bf16[2,64,128,640]{2,3,1,0:T(8,128)(2,1)} fusion(bf16[2,64,128,384]{3,2,1,0:T(8,128)(2,1)} %param.9, bf16[1,384,640]{1,2,0:T(8,128)(2,1)S(1)} %fusion.85, bf16[1,384,640]{1,2,0:T(8,128)(2,1)S(1)} %fusion.82), kind=kOutput, calls=%fused_computation.4 | convolution fusion | flops 8065515520 | bytes 34537472 | tf_op jit(solution)/shard_map/lpmb,lbk->lpmk/dot_general | solution.py:72
  78.9 10.1 %select_convert_fusion.2 = bf16[2,128,64,384]{3,1,2,0:T(8,128)(2,1)} fusion(pred[2,384]{1,0:T(4,128)(4,1)S(1)} %bitcast.232, bf16[2,64,128,640]{2,3,1,0:T(8,128)(2,1)} %convert_bitcast_fusion, bf16[1,128,3,128]{1,3,0,2:T(8,128)(2,1)S(1)} %and_select_fusion.7, bf16[1,128,3,128]{1,3,0,2:T(8,128)(2,1)S(1)} %and_select_fusion.6), kind=kOutput, calls=%fused_computation.3 | convolution fusion | flops 1623326720 | bytes 25363200 | tf_op jit(solution)/shard_map/lmj,lpmc->ljpc/dot_general | solution.py:76
  89.0 10.9 %fusion.108 = (bf16[1,128,64,384]{3,1,2,0:T(8,128)(2,1)}, bf16[1,128,64,384]{3,1,2,0:T(8,128)(2,1)}) fusion(bf16[2,128,64,384]{3,1,2,0:T(8,128)(2,1)} %select_convert_fusion.2), kind=kLoop, calls=%fused_computation.154 | loop fusion | bytes 25165824 | tf_op jit(solution)/shard_map/slice | solution.py:86
  99.9 9.1 %select_convert_fusion = bf16[2,128,64,384]{3,1,2,0:T(8,128)(2,1)} fusion(pred[2,384]{1,0:T(4,128)(4,1)S(1)} %bitcast.231, bf16[2,64,128,640]{2,3,1,0:T(8,128)(2,1)} %convert_bitcast_fusion, bf16[1,128,3,128]{1,3,0,2:T(8,128)(2,1)S(1)} %and_select_fusion.6, bf16[1,128,3,128]{1,3,0,2:T(8,128)(2,1)S(1)} %and_select_fusion.7), kind=kOutput, calls=%fused_computation.1 | convolution fusion | flops 1623326720 | bytes 25363200 | tf_op jit(solution)/shard_map/lmj,lpmc->ljpc/dot_general | solution.py:76
  109.0 10.7 %fusion.109 = (bf16[1,128,64,384]{3,1,2,0:T(8,128)(2,1)}, bf16[1,128,64,384]{3,1,2,0:T(8,128)(2,1)}) fusion(bf16[2,128,64,384]{3,1,2,0:T(8,128)(2,1)} %select_convert_fusion), kind=kLoop, calls=%fused_computation.155 | loop fusion | bytes 25165824 | tf_op jit(solution)/shard_map/slice | solution.py:91
  119.7 1.7 collective-permute-start.3
  121.4 1.5 copy.161
  123.1 9.3 %fusion = bf16[2,128,1,64,384]{4,1,3,0,2:T(8,128)(2,1)} fusion(pred[2,384]{1,0:T(4,128)(4,1)S(1)} %bitcast.230, bf16[2,64,128,640]{2,3,1,0:T(8,128)(2,1)} %convert_bitcast_fusion, bf16[1,128,3,128]{1,3,0,2:T(8,128)(2,1)S(1)} %and_select_fusion.7, bf16[1,128,3,128]{1,3,0,2:T(8,128)(2,1)S(1)} %and_select_fusion.6), kind=kOutput, calls=%fused_computation.5 | convolution fusion | flops 1623326720 | bytes 25363200 | tf_op jit(solution)/shard_map/lmj,lpmc->ljpc/dot_general | solution.py:76
  132.4 105.6 %collective-permute-done.2 = bf16[1,128,64,384]{3,1,2,0:T(8,128)(2,1)} collective-permute-done((bf16[1,128,64,384]{3,1,2,0:T(8,128)(2,1)}, bf16[1,128,64,384]{3,1,2,0:T(8,128)(2,1)}, u32[]{:S(2)}, u32[]{:S(2)}) %collective-permute-start.2) | collective-permute-done | bytes 6291488 | tf_op jit(solution)/shard_map/ppermute | solution.py:12
  238.0 8.5 %maximum_bitcast_fusion = bf16[2,128,1,64,384]{4,1,3,0,2:T(8,128)(2,1)} fusion(bf16[1,128,64,384]{3,1,2,0:T(8,128)(2,1)S(1)} %bitcast.221, bf16[1,128,64,384]{3,1,2,0:T(8,128)(2,1)} %collective-permute-done.2), kind=kLoop, calls=%fused_computation.12 | loop fusion | flops 6291456 | bytes 25165824 | tf_op jit(solution)/shard_map/stack | solution.py:92
  246.5 10.5 %maximum_bitcast_fusion.1 = bf16[2,128,1,64,384]{4,1,3,0,2:T(8,128)(2,1)} fusion(bf16[1,128,64,384]{3,1,2,0:T(8,128)(2,1)} %collective-permute-done.3, bf16[1,128,64,384]{3,1,2,0:T(8,128)(2,1)} %get-tuple-element.22), kind=kLoop, calls=%fused_computation.13 | loop fusion | flops 6291456 | bytes 25165824 | tf_op jit(solution)/shard_map/stack | solution.py:92
  257.0 25.6 %pad_maximum_fusion = bf16[2,128,3,64,384]{4,1,3,0,2:T(8,128)(2,1)} fusion(bf16[2,128,1,64,384]{4,1,3,0,2:T(8,128)(2,1)} %maximum_bitcast_fusion.1, bf16[2,128,1,64,384]{4,1,3,0,2:T(8,128)(2,1)} %fusion, bf16[2,128,1,64,384]{4,1,3,0,2:T(8,128)(2,1)} %maximum_bitcast_fusion), kind=kLoop, calls=%fused_computation | loop fusion | flops 37748736 | bytes 75497472 | tf_op jit(solution)/shard_map/stack | solution.py:92
  282.7 9.4 %pad_maximum_fusion.2 = (bf16[2,16,3,64,384]{4,1,3,0,2:T(8,128)(2,1)}, bf16[2,16,3,64,384]{4,1,3,0,2:T(8,128)(2,1)}) fusion(bf16[2,128,1,64,384]{4,1,3,0,2:T(8,128)(2,1)} %maximum_bitcast_fusion.1, bf16[2,128,1,64,384]{4,1,3,0,2:T(8,128)(2,1)} %fusion, bf16[2,128,1,64,384]{4,1,3,0,2:T(8,128)(2,1)} %maximum_bitcast_fusion), kind=kLoop, calls=%fused_computation.27 | loop fusion | flops 28311552 | bytes 47185920 | tf_op jit(solution)/shard_map/slice | solution.py:98
  292.1 8.7 %copy-done = bf16[2,128,3,64,384]{4,1,3,0,2:T(8,128)(2,1)S(1)} copy-done((bf16[2,128,3,64,384]{4,1,3,0,2:T(8,128)(2,1)S(1)}, bf16[2,128,3,64,384]{4,1,3,0,2:T(8,128)(2,1)}, u32[]{:S(2)}) %copy-start) | copy-done | bytes 37748760
  300.7 10.6 %fusion.105 = (bf16[2,48,3,64,384]{4,1,3,0,2:T(8,128)(2,1)}, bf16[2,48,3,64,384]{4,1,3,0,2:T(8,128)(2,1)}) fusion(bf16[2,128,3,64,384]{4,1,3,0,2:T(8,128)(2,1)S(1)} %copy-done), kind=kLoop, calls=%fused_computation.151 | loop fusion | bytes 56623104 | tf_op jit(solution)/shard_map/slice | solution.py:98
  311.3 5.2 %fusion.38 = f32[2,3,64,64]{2,3,1,0:T(8,128)S(1)} fusion(bf16[4,16,64,384]{3,2,1,0:T(8,128)(2,1)} %all-gather.15.cloned.1.call-done, bf16[2,16,3,64,384]{4,1,3,0,2:T(8,128)(2,1)} %get-tuple-element.13), kind=kOutput, calls=%fused_computation.49 | convolution fusion | flops 301989888 | bytes 6389760 | tf_op jit(solution)/shard_map/lrqc,lropc->lqop/dot_general | solution.py:97
  316.5 5.0 %fusion.35 = f32[2,3,64,64]{2,3,1,0:T(8,128)S(1)} fusion(bf16[4,16,64,384]{3,2,1,0:T(8,128)(2,1)} %all-gather.15.cloned.1.call-done, bf16[2,16,3,64,384]{4,1,3,0,2:T(8,128)(2,1)} %get-tuple-element.13), kind=kOutput, calls=%fused_computation.48 | convolution fusion | flops 301989888 | bytes 6389760 | tf_op jit(solution)/shard_map/lrqc,lropc->lqop/dot_general | solution.py:97
  321.6 11.9 %fusion.41 = f32[2,3,64,64]{2,3,1,0:T(8,128)S(1)} fusion(bf16[4,48,64,384]{3,2,1,0:T(8,128)(2,1)} %all-gather.11.cloned.1.call-done, bf16[2,48,3,64,384]{4,1,3,0,2:T(8,128)(2,1)} %get-tuple-element.14), kind=kOutput, calls=%fused_computation.50 | convolution fusion | flops 905969664 | bytes 18972672 | tf_op jit(solution)/shard_map/lrqc,lropc->lqop/dot_general | solution.py:97
  333.5 7.6 %fusion.44 = f32[2,3,64,64]{2,3,1,0:T(8,128)S(1)} fusion(bf16[4,48,64,384]{3,2,1,0:T(8,128)(2,1)} %all-gather.11.cloned.1.call-done, bf16[2,48,3,64,384]{4,1,3,0,2:T(8,128)(2,1)S(1)} %bitcast.225), kind=kOutput, calls=%fused_computation.51 | convolution fusion | flops 905969664 | bytes 18972672 | tf_op jit(solution)/shard_map/lrqc,lropc->lqop/dot_general | solution.py:97
  341.1 12.4 %fusion.47 = f32[2,3,64,64]{2,3,1,0:T(8,128)S(1)} fusion(bf16[4,48,64,384]{3,2,1,0:T(8,128)(2,1)} %all-gather.13.cloned.1.call-done, bf16[2,48,3,64,384]{4,1,3,0,2:T(8,128)(2,1)} %get-tuple-element.15), kind=kOutput, calls=%fused_computation.52 | convolution fusion | flops 905969664 | bytes 18972672 | tf_op jit(solution)/shard_map/lrqc,lropc->lqop/dot_general | solution.py:97
  353.5 10.7 %fusion.50 = f32[2,3,64,64]{2,3,1,0:T(8,128)S(1)} fusion(bf16[4,48,64,384]{3,2,1,0:T(8,128)(2,1)S(1)} %copy-done.7, bf16[2,48,3,64,384]{4,1,3,0,2:T(8,128)(2,1)} %get-tuple-element.15), kind=kOutput, calls=%fused_computation.53 | convolution fusion | flops 905969664 | bytes 18972672 | tf_op jit(solution)/shard_map/lrqc,lropc->lqop/dot_general | solution.py:97
  364.3 4.8 %fusion.68 = f32[2,3,64,64]{2,3,1,0:T(8,128)S(1)} fusion(f32[2,3,64,64]{2,3,1,0:T(8,128)S(1)} %fusion.38, f32[2,3,64,64]{2,3,1,0:T(8,128)S(1)} %fusion.50, f32[2,3,64,64]{2,3,1,0:T(8,128)S(1)} %fusion.44, bf16[4,16,64,384]{3,2,1,0:T(8,128)(2,1)} %all-gather.9.cloned.1.call-done, bf16[2,16,3,64,384]{4,1,3,0,2:T(8,128)(2,1)} %get-tuple-element.12), kind=kOutput, calls=%fused_computation.59 | convolution fusion | flops 302063616 | bytes 6684672 | tf_op jit(solution)/shard_map/lrqc,lropc->lqop/dot_general | solution.py:97
  369.1 4.8 %select_bitcast_fusion.1 = (f32[2,64,3,64]{3,1,2,0:T(8,128)S(1)}, f32[2,64,3,64]{3,1,2,0:T(8,128)S(1)}) fusion(f32[2,3,64,64]{2,3,1,0:T(8,128)S(1)} %fusion.68, pred[]{:T(512)S(6)} %eq.9, f32[2,3,64,64]{2,3,1,0:T(8,128)S(1)} %fusion.35, f32[2,3,64,64]{2,3,1,0:T(8,128)S(1)} %fusion.47, f32[2,3,64,64]{2,3,1,0:T(8,128)S(1)} %fusion.41, ...), kind=kOutput, calls=%fused_computation.86 | convolution fusion | flops 302112768 | bytes 6881281 | tf_op jit(solution)/shard_map/lrqc,lropc->lqop/dot_general | solution.py:97
  374.0 0.6 collective-permute-start.4
  374.6 5.2 %collective-permute-done.4 = f32[2,64,3,64]{3,1,2,0:T(8,128)S(1)} collective-permute-done((f32[2,64,3,64]{3,1,2,0:T(8,128)S(1)}, f32[2,64,3,64]{3,1,2,0:T(8,128)S(1)}, u32[]{:S(2)}, u32[]{:S(2)}) %collective-permute-start.4) | collective-permute-done | bytes 98336 | tf_op jit(solution)/shard_map/ppermute | solution.py:12
  379.7 0.9 copy_bitcast_fusion.4
  (69 shorter events, 1.7 us)
Async XLA Ops:
  6.5 304.8 %all-gather.15.cloned.1.call-start = ((), (), s32[]{:S(2)}) async-start(), calls=%async_computation.3 | async-start | bytes 4718592 | tf_op jit(solution)/shard_map/all_gather | solution.py:29
  10.3 311.2 %all-gather.11.cloned.1.call-start = ((), (), s32[]{:S(2)}) async-start(), calls=%async_computation.1 | async-start | bytes 14155776 | tf_op jit(solution)/shard_map/all_gather | solution.py:29
  17.3 3.6 copy-start.1
  17.3 11.7 %copy-start.4 = (s32[32,3]{0,1:T(4,128)S(1)}, s32[32,3]{0,1:T(4,128)}, u32[]{:S(2)}) copy-start(s32[32,3]{0,1:T(4,128)} %param.14) | copy-start | bytes 1156
  17.3 11.7 %copy-start.5 = (s32[32,3]{0,1:T(4,128)S(1)}, s32[32,3]{0,1:T(4,128)}, u32[]{:S(2)}) copy-start(s32[32,3]{0,1:T(4,128)} %param.13) | copy-start | bytes 1156
  17.3 11.9 %copy-start.3 = (s32[32,3]{0,1:T(4,128)S(1)}, s32[32,3]{0,1:T(4,128)}, u32[]{:S(2)}) copy-start(s32[32,3]{0,1:T(4,128)} %param.12) | copy-start | bytes 1156
  17.3 12.2 %copy-start.6 = (s32[32]{0:T(128)S(1)}, s32[32]{0:T(128)}, u32[]{:S(2)}) copy-start(s32[32]{0:T(128)} %param.15) | copy-start | bytes 388
  20.7 20.5 %copy-start.2 = (bf16[128,384]{1,0:T(8,128)(2,1)S(1)}, bf16[128,384]{1,0:T(8,128)(2,1)}, u32[]{:S(2)}) copy-start(bf16[128,384]{1,0:T(8,128)(2,1)} %param.10) | copy-start | bytes 294916
  20.8 320.4 %all-gather.13.cloned.1.call-start = ((), (), s32[]{:S(2)}) async-start(), calls=%async_computation.2 | async-start | bytes 14155776 | tf_op jit(solution)/shard_map/all_gather | solution.py:29
  33.5 18.0 %collective-permute-start = (bf16[1,128,384]{1,2,0:T(8,128)(2,1)S(1)}, bf16[1,128,384]{1,2,0:T(8,128)(2,1)S(1)}, u32[]{:S(2)}, u32[]{:S(2)}) collective-permute-start(bf16[1,128,384]{1,2,0:T(8,128)(2,1)S(1)} %get-tuple-element.33), channel_id=1, source_target_pairs={{0,2},{2,4},{4,6},{6,8},{8,10},{10,12},{12,14},{14,16},{16,18},{18... | collective-permute-start | bytes 294920 | tf_op jit(solution)/shard_map/ppermute | solution.py:12
  33.6 18.1 %collective-permute-start.1 = (bf16[1,128,384]{1,2,0:T(8,128)(2,1)S(1)}, bf16[1,128,384]{1,2,0:T(8,128)(2,1)S(1)}, u32[]{:S(2)}, u32[]{:S(2)}) collective-permute-start(bf16[1,128,384]{1,2,0:T(8,128)(2,1)S(1)} %get-tuple-element.36), channel_id=1, source_target_pairs={{0,30},{2,0},{4,2},{6,4},{8,6},{10,8},{12,10},{14,12},{16,14},{18,... | collective-permute-start | bytes 294920 | tf_op jit(solution)/shard_map/ppermute | solution.py:12
  41.1 323.2 %all-gather.9.cloned.1.call-start = ((), (), s32[]{:S(2)}) async-start(), calls=%async_computation | async-start | bytes 4718592 | tf_op jit(solution)/shard_map/all_gather | solution.py:29
  99.9 138.1 %collective-permute-start.2 = (bf16[1,128,64,384]{3,1,2,0:T(8,128)(2,1)}, bf16[1,128,64,384]{3,1,2,0:T(8,128)(2,1)}, u32[]{:S(2)}, u32[]{:S(2)}) collective-permute-start(bf16[1,128,64,384]{3,1,2,0:T(8,128)(2,1)} %get-tuple-element.20), channel_id=1, source_target_pairs={{0,2},{2,4},{4,6},{6,8},{8,10},{10,12},{12,14},{14,16},{16,18},{18... | collective-permute-start | bytes 18874376 | tf_op jit(solution)/shard_map/ppermute | solution.py:12
  119.7 126.9 %collective-permute-start.3 = (bf16[1,128,64,384]{3,1,2,0:T(8,128)(2,1)}, bf16[1,128,64,384]{3,1,2,0:T(8,128)(2,1)}, u32[]{:S(2)}, u32[]{:S(2)}) collective-permute-start(bf16[1,128,64,384]{3,1,2,0:T(8,128)(2,1)} %get-tuple-element.23), channel_id=1, source_target_pairs={{0,30},{2,0},{4,2},{6,4},{8,6},{10,8},{12,10},{14,12},{16,14},{18,... | collective-permute-start | bytes 18874376 | tf_op jit(solution)/shard_map/ppermute | solution.py:12
  122.9 115.1 %slice-start = ((s8[6291456]{0:T(1024)(128)(4,1)}), s8[2097152]{0:T(1024)(128)(4,1)S(1)}, s32[]{:S(2)}) async-start(s8[6291456]{0:T(1024)(128)(4,1)} %bitcast.220), calls=%async_computation.4 | async-start | bytes 4194304
  123.1 114.9 %slice-start.1 = ((s8[6291456]{0:T(1024)(128)(4,1)}), s8[4194304]{0:T(1024)(128)(4,1)S(1)}, s32[]{:S(2)}) async-start(s8[6291456]{0:T(1024)(128)(4,1)} %bitcast.220), calls=%async_computation.5 | async-start | bytes 8388608
  282.7 18.1 %copy-start = (bf16[2,128,3,64,384]{4,1,3,0,2:T(8,128)(2,1)S(1)}, bf16[2,128,3,64,384]{4,1,3,0,2:T(8,128)(2,1)}, u32[]{:S(2)}) copy-start(bf16[2,128,3,64,384]{4,1,3,0,2:T(8,128)(2,1)} %pad_maximum_fusion) | copy-start | bytes 113246208
  316.5 16.9 %slice-start.2 = ((s8[14155776]{0:T(1024)(128)(4,1)}), s8[1572864]{0:T(1024)(128)(4,1)S(1)}, s32[]{:S(2)}) async-start(s8[14155776]{0:T(1024)(128)(4,1)} %bitcast.224), calls=%async_computation.6 | async-start | bytes 3145728
  321.5 11.9 %slice-start.3 = ((s8[14155776]{0:T(1024)(128)(4,1)}), s8[4194304]{0:T(1024)(128)(4,1)S(1)}, s32[]{:S(2)}) async-start(s8[14155776]{0:T(1024)(128)(4,1)} %bitcast.224), calls=%async_computation.7 | async-start | bytes 8388608
  321.5 11.9 %slice-start.4 = ((s8[14155776]{0:T(1024)(128)(4,1)}), s8[4194304]{0:T(1024)(128)(4,1)S(1)}, s32[]{:S(2)}) async-start(s8[14155776]{0:T(1024)(128)(4,1)} %bitcast.224), calls=%async_computation.8 | async-start | bytes 8388608
  321.6 11.9 %slice-start.5 = ((s8[14155776]{0:T(1024)(128)(4,1)}), s8[4194304]{0:T(1024)(128)(4,1)S(1)}, s32[]{:S(2)}) async-start(s8[14155776]{0:T(1024)(128)(4,1)} %bitcast.224), calls=%async_computation.9 | async-start | bytes 8388608
  341.1 12.4 %copy-start.7 = (bf16[4,48,64,384]{3,2,1,0:T(8,128)(2,1)S(1)}, bf16[4,48,64,384]{3,2,1,0:T(8,128)(2,1)}, u32[]{:S(2)}) copy-start(bf16[4,48,64,384]{3,2,1,0:T(8,128)(2,1)} %all-gather.13.cloned.1.call-done) | copy-start | bytes 28311556
  374.0 5.7 %collective-permute-start.4 = (f32[2,64,3,64]{3,1,2,0:T(8,128)S(1)}, f32[2,64,3,64]{3,1,2,0:T(8,128)S(1)}, u32[]{:S(2)}, u32[]{:S(2)}) collective-permute-start(f32[2,64,3,64]{3,1,2,0:T(8,128)S(1)} %get-tuple-element.25), channel_id=1, source_target_pairs={{0,1},{1,0},{2,3},{3,2},{4,5},{5,4},{6,7},{7,6},{8,9},{9,8},{10,11... | collective-permute-start | bytes 294920 | tf_op jit(solution)/shard_map/ppermute | solution.py:12
Sparse Core Ops, SparseCore 0:
  10.4 49.4 all-gather.14
  61.4 117.9 all-gather.10
  181.0 117.9 all-gather.12
  300.5 44.9 all-gather.8

commit v2 on v1

--- a/solution.py
+++ b/solution.py
@@ -3,7 +3,7 @@
 from jax import lax
 from jax.sharding import PartitionSpec as P
 
-CHUNKS = (16, 48, 48, 16)
+CHUNKS = (16, 72)
 
 
 def shift(value, axis, steps):
@@ -26,6 +26,8 @@
         bounds.append((low, low + rows))
         low += rows
     local = [three[:, :, lo:hi].transpose(0, 2, 1, 3) for lo, hi in bounds]
+    rest = three[:, :, low:].transpose(0, 2, 1, 3)
+    rest_other = shift(rest, "aux", 1)
     both = [lax.all_gather(piece, "aux", axis=0, tiled=False) for piece in local]
 
     vir_rows = lax.all_gather(virtual, "aux", axis=0, tiled=True)
@@ -103,6 +105,9 @@
     parts = [contract([piece[s] for piece in both]) for s in range(2)]
     own = jnp.where(side == 0, parts[0], parts[1])
     cross = jnp.where(side == 0, parts[1], parts[0])
+    tail = sources[:, low:]
+    own = own + jnp.einsum("lrqc,lropc->lqop", rest, tail, preferred_element_type=f32)
+    cross = cross + jnp.einsum("lrqc,lropc->lqop", rest_other, tail, preferred_element_type=f32)
     got = shift(cross, "aux", 1)
     sides = jnp.where(
         side == 0,

time: 388 us -> 369 us (0.951)
  waiting for transfers between devices: 111 us -> 103 us
  matrix products: 118 us -> 111 us
  blocking collectives: 16 us -> 11.4 us
  other arithmetic: 59.8 us -> 64.1 us
  local copies, waits for them, and re-layouts: 64.6 us -> 60.7 us
    dot_general x8 -> x4, matrix products: 62.4 us -> 34 us  [contract(): jnp.einsum('lrqc,lropc->lqop', piece, sources[:, lo:hi], preferred_elemen...]
    dot_general x0 -> x2, matrix products: none -> 20.5 us  [the longest x1 10.3 us: shards(): jnp.einsum('lrqc,lropc->lqop', rest, tail, preferred_element_type=f32)]
    unnamed x39 -> x40, local copies, waits for them, and re-layouts: 21.3 us -> 10.6 us
    slice x1, local copies, waits for them, and re-layouts: 10.6 us -> 21.2 us  [contract(): sources[:, lo:hi]]
    slice x0 -> x1, other arithmetic: none -> 8.06 us  [shards(): tail = sources[:, low:]]
    ppermute x5 -> x6, waiting for transfers between devices: 111 us -> 103 us  [shift(): return lax.ppermute(value, axis, pairs)]
    slice x2 -> x4, local copies, waits for them, and re-layouts: 9.18 us -> 3.01 us  [shards(): local = [three[:, :, lo:hi].transpose(0, 2, 1, 3) for lo, hi in bounds]]
    slice x1, other arithmetic: 9.38 us -> 5.41 us  [contract(): sources[:, lo:hi]]
  transfers between devices with their start and end apart: 9 -> 8, of which waited for: 2 -> 2; matrix products, arithmetic and copies ran while one was open for 57% -> 56% of each run, Pallas kernels for 0% -> 0%
where the time goes in v2:
time: 369 us; the launch traced here: 366 us
  matrix products  111 us (30%)
  waiting for transfers between devices  103 us (28%)
  other arithmetic  64.1 us (17%)
  local copies, waits for them, and re-layouts  60.7 us (16%)
  between operations  13.8 us (4%)
  blocking collectives  11.4 us (3%)
    ppermute x6, waiting for transfers between devices, shift(): return lax.ppermute(value, axis, pairs)  103 us
    another operation x3, other arithmetic, shards(): sources = jnp.stack([before, mid, after], axis=2)  44.9 us
    dot_general x4, matrix products, contract(): jnp.einsum('lrqc,lropc->lqop', piece, sources[:, lo:hi], preferred_elemen...  34 us
    dot_general x1, matrix products, shards(): jnp.einsum('lpmb,lbk->lpmk', three, band, preferred_element_type=f32)  28.2 us
    dot_general x3, matrix products, pair(): jnp.einsum('lmj,lpmc->ljpc', density[:, :, t], mixed[:, :, :, t * width:(...  27.8 us
    slice x1, local copies, waits for them, and re-layouts, contract(): sources[:, lo:hi]  21.2 us
    slice x1, local copies, waits for them, and re-layouts, shards(): from_left = shift(up[-1:], 'atom', 1)  10.8 us
    slice x1, local copies, waits for them, and re-layouts, shards(): after = jnp.concatenate([down[1:], from_right], axis=0)  10.7 us
  transfers between devices with their start and end apart: 8, of which 2 were waited for; matrix products, arithmetic and copies ran while one was open for 56% of the time, Pallas kernels for 0%

profile of v2, /device:TPU:6, one launch (start us, length us, event | category | flops | bytes accessed | tf_op | source)
XLA Modules:
  0.0 366.2 jit_solution(8586865605335645745)
XLA Ops:
  6.5 3.0 slice-done.6
  9.6 4.3 %copy.139 = bf16[2,64,72,384]{3,1,2,0:T(8,128)(2,1)} copy(bf16[2,64,72,384]{3,2,1,0:T(8,128)(2,1)S(1)} %slice-done.6) | data formatting | bytes 14155776
  14.5 0.1 copy.50
  14.6 5.3 %all_gather.19 = bf16[256,384]{0,1:T(8,128)(2,1)S(1)} all-gather(bf16[128,384]{0,1:T(8,128)(2,1)S(1)} %copy.50), channel_id=1, replica_groups=mesh['atom'=16,'aux'=2] {'aux'}, dimensions={0}, use_global_device_ids=true | all-gather | bytes 294912 | tf_op jit(solution)/shard_map/all_gather | solution.py:33
  20.1 0.2 slice_reduce_fusion.5
  20.3 0.2 slice_reduce_fusion.3
  20.5 0.6 fusion.94
  21.2 2.4 broadcast_and_fusion.3
  23.6 0.2 and_select_fusion.4
  23.9 0.5 collective-permute-start
  24.6 6.1 %all_gather.18 = bf16[256,384]{1,0:T(8,128)(2,1)S(1)} all-gather(bf16[128,384]{1,0:T(8,128)(2,1)S(1)} %copy-done.2), channel_id=1, replica_groups=mesh['atom'=16,'aux'=2] {'aux'}, dimensions={0}, use_global_device_ids=true | all-gather | bytes 294912 | tf_op jit(solution)/shard_map/all_gather | solution.py:34
  30.7 0.1 copy.49
  30.8 0.1 copy.48
  31.0 0.1 copy.47
  31.1 1.3 slice_bitcast_fusion.23
  32.4 0.1 and_select_fusion.6
  32.6 0.1 and_select_fusion.7
  32.8 0.1 and_select_fusion
  33.0 0.1 and_select_fusion.5
  33.2 28.2 %convert_bitcast_fusion = bf16[2,64,128,640]{2,3,1,0:T(8,128)(2,1)} fusion(bf16[2,64,128,384]{3,2,1,0:T(8,128)(2,1)} %param.9, bf16[1,384,640]{1,2,0:T(8,128)(2,1)S(1)} %fusion.70, bf16[1,384,640]{1,2,0:T(8,128)(2,1)S(1)} %fusion.67), kind=kOutput, calls=%fused_computation.4 | convolution fusion | flops 8065515520 | bytes 34537472 | tf_op jit(solution)/shard_map/lpmb,lbk->lpmk/dot_general | solution.py:74
  61.4 9.1 %select_convert_fusion = bf16[2,128,64,384]{3,1,2,0:T(8,128)(2,1)} fusion(pred[2,384]{1,0:T(4,128)(4,1)S(1)} %bitcast.193, bf16[2,64,128,640]{2,3,1,0:T(8,128)(2,1)} %convert_bitcast_fusion, bf16[1,128,3,128]{1,3,0,2:T(8,128)(2,1)S(1)} %and_select_fusion.6, bf16[1,128,3,128]{1,3,0,2:T(8,128)(2,1)S(1)} %and_select_fusion.7), kind=kOutput, calls=%fused_computation.1 | convolution fusion | flops 1623326720 | bytes 25363200 | tf_op jit(solution)/shard_map/lmj,lpmc->ljpc/dot_general | solution.py:78
  70.5 10.7 %fusion.91 = (bf16[1,128,64,384]{3,1,2,0:T(8,128)(2,1)}, bf16[1,128,64,384]{3,1,2,0:T(8,128)(2,1)}) fusion(bf16[2,128,64,384]{3,1,2,0:T(8,128)(2,1)} %select_convert_fusion), kind=kLoop, calls=%fused_computation.140 | loop fusion | bytes 25165824 | tf_op jit(solution)/shard_map/slice | solution.py:93
  81.1 9.1 %select_convert_fusion.2 = bf16[2,128,64,384]{3,1,2,0:T(8,128)(2,1)} fusion(pred[2,384]{1,0:T(4,128)(4,1)S(1)} %bitcast.192, bf16[2,64,128,640]{2,3,1,0:T(8,128)(2,1)} %convert_bitcast_fusion, bf16[1,128,3,128]{1,3,0,2:T(8,128)(2,1)S(1)} %and_select_fusion.7, bf16[1,128,3,128]{1,3,0,2:T(8,128)(2,1)S(1)} %and_select_fusion.6), kind=kOutput, calls=%fused_computation.3 | convolution fusion | flops 1623326720 | bytes 25363200 | tf_op jit(solution)/shard_map/lmj,lpmc->ljpc/dot_general | solution.py:78
  90.2 10.8 %fusion.90 = (bf16[1,128,64,384]{3,1,2,0:T(8,128)(2,1)}, bf16[1,128,64,384]{3,1,2,0:T(8,128)(2,1)}) fusion(bf16[2,128,64,384]{3,1,2,0:T(8,128)(2,1)} %select_convert_fusion.2), kind=kLoop, calls=%fused_computation.139 | loop fusion | bytes 25165824 | tf_op jit(solution)/shard_map/slice | solution.py:88
  101.1 0.5 collective-permute-start.2
  101.6 2.5 slice.238
  104.1 3.1 copy.140
  107.2 0.5 collective-permute-start.4
  107.8 1.5 copy.141
  109.4 0.1 copy.52
  109.6 9.7 %fusion.4 = bf16[2,128,1,64,384]{4,1,3,0,2:T(8,128)(2,1)} fusion(pred[2,384]{1,0:T(4,128)(4,1)S(1)} %bitcast.191, bf16[2,64,128,640]{2,3,1,0:T(8,128)(2,1)} %convert_bitcast_fusion, bf16[1,128,3,128]{1,3,0,2:T(8,128)(2,1)S(1)} %and_select_fusion.7, bf16[1,128,3,128]{1,3,0,2:T(8,128)(2,1)S(1)} %and_select_fusion.6), kind=kOutput, calls=%fused_computation.9 | convolution fusion | flops 1623326720 | bytes 25363200 | tf_op jit(solution)/shard_map/lmj,lpmc->ljpc/dot_general | solution.py:78
  119.2 98.2 %collective-permute-done.3 = bf16[1,128,64,384]{3,1,2,0:T(8,128)(2,1)} collective-permute-done((bf16[1,128,64,384]{3,1,2,0:T(8,128)(2,1)}, bf16[1,128,64,384]{3,1,2,0:T(8,128)(2,1)}, u32[]{:S(2)}, u32[]{:S(2)}) %collective-permute-start.3) | collective-permute-done | bytes 6291488 | tf_op jit(solution)/shard_map/ppermute | solution.py:12
  217.4 8.5 %maximum_bitcast_fusion.1 = bf16[2,128,1,64,384]{4,1,3,0,2:T(8,128)(2,1)} fusion(bf16[1,128,64,384]{3,1,2,0:T(8,128)(2,1)} %collective-permute-done.3, bf16[1,128,64,384]{3,1,2,0:T(8,128)(2,1)S(1)} %bitcast.187), kind=kLoop, calls=%fused_computation.17 | loop fusion | flops 6291456 | bytes 25165824 | tf_op jit(solution)/shard_map/stack | solution.py:94
  225.8 10.6 %maximum_bitcast_fusion = bf16[2,128,1,64,384]{4,1,3,0,2:T(8,128)(2,1)} fusion(bf16[1,128,64,384]{3,1,2,0:T(8,128)(2,1)} %get-tuple-element.13, bf16[1,128,64,384]{3,1,2,0:T(8,128)(2,1)} %collective-permute-done.2), kind=kLoop, calls=%fused_computation.16 | loop fusion | flops 6291456 | bytes 25165824 | tf_op jit(solution)/shard_map/stack | solution.py:94
  236.5 25.8 %pad_maximum_fusion = bf16[2,128,3,64,384]{4,1,3,0,2:T(8,128)(2,1)} fusion(bf16[2,128,1,64,384]{4,1,3,0,2:T(8,128)(2,1)} %maximum_bitcast_fusion.1, bf16[2,128,1,64,384]{4,1,3,0,2:T(8,128)(2,1)} %fusion.4, bf16[2,128,1,64,384]{4,1,3,0,2:T(8,128)(2,1)} %maximum_bitcast_fusion), kind=kLoop, calls=%fused_computation | loop fusion | flops 37748736 | bytes 75497472 | tf_op jit(solution)/shard_map/stack | solution.py:94
  262.3 21.2 %slice.267 = bf16[2,72,3,64,384]{4,1,3,0,2:T(8,128)(2,1)} slice(bf16[2,128,3,64,384]{4,1,3,0,2:T(8,128)(2,1)} %pad_maximum_fusion), slice={[0:2], [16:88], [0:3], [0:64], [0:384]} | slice | bytes 42467328 | tf_op jit(solution)/shard_map/slice | solution.py:100
  283.5 5.4 %pad_maximum_fusion.2 = bf16[2,16,3,64,384]{4,1,3,0,2:T(8,128)(2,1)} fusion(bf16[2,128,1,64,384]{4,1,3,0,2:T(8,128)(2,1)} %maximum_bitcast_fusion.1, bf16[2,128,1,64,384]{4,1,3,0,2:T(8,128)(2,1)} %fusion.4, bf16[2,128,1,64,384]{4,1,3,0,2:T(8,128)(2,1)} %maximum_bitcast_fusion), kind=kLoop, calls=%fused_computation.26 | loop fusion | flops 14155776 | bytes 42467328 | tf_op jit(solution)/shard_map/slice | solution.py:100
  288.9 1.2 slice-done.5
  290.1 8.1 %pad_maximum_fusion.1 = bf16[2,40,3,64,384]{4,1,3,0,2:T(8,128)(2,1)} fusion(bf16[2,128,1,64,384]{4,1,3,0,2:T(8,128)(2,1)S(1)} %bitcast.184, bf16[2,128,1,64,384]{4,1,3,0,2:T(8,128)(2,1)S(1)} %bitcast.182, bf16[2,128,1,64,384]{4,1,3,0,2:T(8,128)(2,1)} %maximum_bitcast_fusion), kind=kLoop, calls=%fused_computation.18 | loop fusion | flops 35389440 | bytes 49545216 | tf_op jit(solution)/shard_map/slice | solution.py:108
  298.1 10.2 %fusion.39 = f32[2,3,64,64]{2,3,1,0:T(8,128)S(1)} fusion(bf16[2,40,64,384]{3,2,1,0:T(8,128)(2,1)} %collective-permute-done.4, bf16[2,40,3,64,384]{4,1,3,0,2:T(8,128)(2,1)} %pad_maximum_fusion.1), kind=kOutput, calls=%fused_computation.43 | convolution fusion | flops 754974720 | bytes 15826944 | tf_op jit(solution)/shard_map/lrqc,lropc->lqop/dot_general | solution.py:110
  308.4 12.1 %fusion.44 = f32[2,3,64,64]{2,3,1,0:T(8,128)S(1)} fusion(bf16[4,72,64,384]{3,2,1,0:T(8,128)(2,1)} %all-gather.7.cloned.1.call-done, bf16[2,72,3,64,384]{4,1,3,0,2:T(8,128)(2,1)} %slice.267), kind=kOutput, calls=%fused_computation.44 | convolution fusion | flops 1358954496 | bytes 28409856 | tf_op jit(solution)/shard_map/lrqc,lropc->lqop/dot_general | solution.py:99
  320.5 12.3 %fusion.47 = f32[2,3,64,64]{2,3,1,0:T(8,128)S(1)} fusion(bf16[4,72,64,384]{3,2,1,0:T(8,128)(2,1)} %all-gather.7.cloned.1.call-done, bf16[2,72,3,64,384]{4,1,3,0,2:T(8,128)(2,1)} %slice.267), kind=kOutput, calls=%fused_computation.45 | convolution fusion | flops 1358954496 | bytes 28409856 | tf_op jit(solution)/shard_map/lrqc,lropc->lqop/dot_general | solution.py:99
  332.8 4.8 %fusion.53 = f32[2,3,64,64]{2,3,1,0:T(8,128)S(1)} fusion(f32[2,3,64,64]{2,3,1,0:T(8,128)S(1)} %fusion.44, bf16[4,16,64,384]{3,2,1,0:T(8,128)(2,1)} %all-gather.5.cloned.1.call-done, bf16[2,16,3,64,384]{4,1,3,0,2:T(8,128)(2,1)} %pad_maximum_fusion.2), kind=kOutput, calls=%fused_computation.47 | convolution fusion | flops 302014464 | bytes 6488064 | tf_op jit(solution)/shard_map/lrqc,lropc->lqop/dot_general | solution.py:99
  337.7 4.8 %fusion.50 = f32[2,3,64,64]{2,3,1,0:T(8,128)S(1)} fusion(f32[2,3,64,64]{2,3,1,0:T(8,128)S(1)} %fusion.47, bf16[4,16,64,384]{3,2,1,0:T(8,128)(2,1)} %all-gather.5.cloned.1.call-done, bf16[2,16,3,64,384]{4,1,3,0,2:T(8,128)(2,1)} %pad_maximum_fusion.2), kind=kOutput, calls=%fused_computation.46 | convolution fusion | flops 302014464 | bytes 6488064 | tf_op jit(solution)/shard_map/lrqc,lropc->lqop/dot_general | solution.py:99
  342.5 10.3 %add_bitcast_fusion.1 = (f32[2,64,3,64]{3,1,2,0:T(8,128)S(1)}, f32[2,64,3,64]{3,1,2,0:T(8,128)S(1)}) fusion(f32[2,3,64,64]{2,3,1,0:T(8,128)S(1)} %fusion.53, f32[2,3,64,64]{2,3,1,0:T(8,128)S(1)} %fusion.50, pred[]{:T(512)S(6)} %eq.9, f32[2,3,64,64]{2,3,1,0:T(8,128)S(1)} %fusion.39, bf16[2,64,40,384]{3,2,1,0:T(8,128)(2,1)} %copy-done, ...), kind=kOutput, calls=%fused_computation.74 | convolution fusion | flops 755073024 | bytes 16220161 | tf_op jit(solution)/shard_map/lrqc,lropc->lqop/dot_general | solution.py:109
  352.8 0.6 collective-permute-start.5
  353.4 5.1 %collective-permute-done.5 = f32[2,64,3,64]{3,1,2,0:T(8,128)S(1)} collective-permute-done((f32[2,64,3,64]{3,1,2,0:T(8,128)S(1)}, f32[2,64,3,64]{3,1,2,0:T(8,128)S(1)}, u32[]{:S(2)}, u32[]{:S(2)}) %collective-permute-start.5) | collective-permute-done | bytes 98336 | tf_op jit(solution)/shard_map/ppermute | solution.py:12
  358.5 0.9 copy_bitcast_fusion.3
  (69 shorter events, 1.5 us)
Async XLA Ops:
  6.5 301.9 %all-gather.7.cloned.1.call-start = ((), (), s32[]{:S(2)}) async-start(), calls=%async_computation.1 | async-start | bytes 21233664 | tf_op jit(solution)/shard_map/all_gather | solution.py:31
  6.5 3.0 slice-start.6
  9.5 4.5 %copy-start.3 = (s32[32,3]{0,1:T(4,128)S(1)}, s32[32,3]{0,1:T(4,128)}, u32[]{:S(2)}) copy-start(s32[32,3]{0,1:T(4,128)} %param.12) | copy-start | bytes 1156
  9.5 4.6 %copy-start.4 = (s32[32,3]{0,1:T(4,128)S(1)}, s32[32,3]{0,1:T(4,128)}, u32[]{:S(2)}) copy-start(s32[32,3]{0,1:T(4,128)} %param.14) | copy-start | bytes 1156
  9.6 4.6 %copy-start.5 = (s32[32,3]{0,1:T(4,128)S(1)}, s32[32,3]{0,1:T(4,128)}, u32[]{:S(2)}) copy-start(s32[32,3]{0,1:T(4,128)} %param.13) | copy-start | bytes 1156
  9.6 4.9 %copy-start.1 = (bf16[128,384]{1,0:T(8,128)(2,1)S(1)}, bf16[128,384]{1,0:T(8,128)(2,1)}, u32[]{:S(2)}) copy-start(bf16[128,384]{1,0:T(8,128)(2,1)} %param.11) | copy-start | bytes 294916
  9.6 10.4 %copy-start.6 = (s32[32]{0:T(128)S(1)}, s32[32]{0:T(128)}, u32[]{:S(2)}) copy-start(s32[32]{0:T(128)} %param.15) | copy-start | bytes 388
  9.6 15.0 %copy-start.2 = (bf16[128,384]{1,0:T(8,128)(2,1)S(1)}, bf16[128,384]{1,0:T(8,128)(2,1)}, u32[]{:S(2)}) copy-start(bf16[128,384]{1,0:T(8,128)(2,1)} %param.10) | copy-start | bytes 294916
  13.9 318.9 %all-gather.5.cloned.1.call-start = ((), (), s32[]{:S(2)}) async-start(), calls=%async_computation | async-start | bytes 4718592 | tf_op jit(solution)/shard_map/all_gather | solution.py:31
  23.8 9.0 %collective-permute-start.1 = (bf16[1,128,384]{1,2,0:T(8,128)(2,1)S(1)}, bf16[1,128,384]{1,2,0:T(8,128)(2,1)S(1)}, u32[]{:S(2)}, u32[]{:S(2)}) collective-permute-start(bf16[1,128,384]{1,2,0:T(8,128)(2,1)S(1)} %get-tuple-element.28), channel_id=1, source_target_pairs={{0,30},{2,0},{4,2},{6,4},{8,6},{10,8},{12,10},{14,12},{16,14},{18,... | collective-permute-start | bytes 294920 | tf_op jit(solution)/shard_map/ppermute | solution.py:12
  23.9 9.1 %collective-permute-start = (bf16[1,128,384]{1,2,0:T(8,128)(2,1)S(1)}, bf16[1,128,384]{1,2,0:T(8,128)(2,1)S(1)}, u32[]{:S(2)}, u32[]{:S(2)}) collective-permute-start(bf16[1,128,384]{1,2,0:T(8,128)(2,1)S(1)} %get-tuple-element.25), channel_id=1, source_target_pairs={{0,2},{2,4},{4,6},{6,8},{8,10},{10,12},{12,14},{14,16},{16,18},{18... | collective-permute-start | bytes 294920 | tf_op jit(solution)/shard_map/ppermute | solution.py:12
  81.1 136.2 %collective-permute-start.3 = (bf16[1,128,64,384]{3,1,2,0:T(8,128)(2,1)}, bf16[1,128,64,384]{3,1,2,0:T(8,128)(2,1)}, u32[]{:S(2)}, u32[]{:S(2)}) collective-permute-start(bf16[1,128,64,384]{3,1,2,0:T(8,128)(2,1)} %get-tuple-element.15), channel_id=1, source_target_pairs={{0,30},{2,0},{4,2},{6,4},{8,6},{10,8},{12,10},{14,12},{16,14},{18,... | collective-permute-start | bytes 18874376 | tf_op jit(solution)/shard_map/ppermute | solution.py:12
  101.1 6.7 %slice-start.7 = ((bf16[2,64,128,384]{3,2,1,0:T(8,128)(2,1)}), bf16[2,64,16,384]{3,2,1,0:T(8,128)(2,1)S(1)}, s32[]{:S(2)}) async-start(bf16[2,64,128,384]{3,2,1,0:T(8,128)(2,1)} %param.9), calls=%async_computation.9 | async-start | bytes 3145728 | tf_op jit(solution)/shard_map/slice | solution.py:28
  101.1 124.8 %collective-permute-start.2 = (bf16[1,128,64,384]{3,1,2,0:T(8,128)(2,1)}, bf16[1,128,64,384]{3,1,2,0:T(8,128)(2,1)}, u32[]{:S(2)}, u32[]{:S(2)}) collective-permute-start(bf16[1,128,64,384]{3,1,2,0:T(8,128)(2,1)} %get-tuple-element.12), channel_id=1, source_target_pairs={{0,2},{2,4},{4,6},{6,8},{8,10},{10,12},{12,14},{14,16},{16,18},{18... | collective-permute-start | bytes 18874376 | tf_op jit(solution)/shard_map/ppermute | solution.py:12
  104.1 5.2 %copy-start = (bf16[2,64,40,384]{3,2,1,0:T(8,128)(2,1)}, bf16[2,64,40,384]{3,2,1,0:T(8,128)(2,1)S(1)}, u32[]{:S(2)}) copy-start(bf16[2,64,40,384]{3,2,1,0:T(8,128)(2,1)S(1)} %slice.238) | copy-start | bytes 11796484
  107.2 190.9 %collective-permute-start.4 = (bf16[2,40,64,384]{3,2,1,0:T(8,128)(2,1)}, bf16[2,40,64,384]{3,2,1,0:T(8,128)(2,1)}, u32[]{:S(2)}, u32[]{:S(2)}) collective-permute-start(bf16[2,40,64,384]{3,2,1,0:T(8,128)(2,1)} %bitcast.176), channel_id=1, source_target_pairs={{0,1},{1,0},{2,3},{3,2},{4,5},{5,4},{6,7},{7,6},{8,9},{9,8},{10,11... | collective-permute-start | bytes 11796488 | tf_op jit(solution)/shard_map/ppermute | solution.py:12
  109.3 108.0 %slice-start.8 = ((s8[6291456]{0:T(1024)(128)(4,1)}), s8[2097152]{0:T(1024)(128)(4,1)S(1)}, s32[]{:S(2)}) async-start(s8[6291456]{0:T(1024)(128)(4,1)} %bitcast.186), calls=%async_computation.10 | async-start | bytes 4194304
  109.6 107.8 %slice-start.9 = ((s8[6291456]{0:T(1024)(128)(4,1)}), s8[4194304]{0:T(1024)(128)(4,1)S(1)}, s32[]{:S(2)}) async-start(s8[6291456]{0:T(1024)(128)(4,1)} %bitcast.186), calls=%async_computation.11 | async-start | bytes 8388608
  262.2 26.6 %slice-start = ((s8[12582912]{0:T(1024)(128)(4,1)}), s8[4194304]{0:T(1024)(128)(4,1)S(1)}, s32[]{:S(2)}) async-start(s8[12582912]{0:T(1024)(128)(4,1)} %bitcast.181), calls=%async_computation.2 | async-start | bytes 8388608
  262.3 26.6 %slice-start.1 = ((s8[12582912]{0:T(1024)(128)(4,1)}), s8[4194304]{0:T(1024)(128)(4,1)S(1)}, s32[]{:S(2)}) async-start(s8[12582912]{0:T(1024)(128)(4,1)} %bitcast.181), calls=%async_computation.3 | async-start | bytes 8388608
  262.3 26.6 %slice-start.3 = ((s8[12582912]{0:T(1024)(128)(4,1)}), s8[4194304]{0:T(1024)(128)(4,1)S(1)}, s32[]{:S(2)}) async-start(s8[12582912]{0:T(1024)(128)(4,1)} %bitcast.183), calls=%async_computation.5 | async-start | bytes 8388608
  262.3 26.6 %slice-start.4 = ((s8[12582912]{0:T(1024)(128)(4,1)}), s8[4194304]{0:T(1024)(128)(4,1)S(1)}, s32[]{:S(2)}) async-start(s8[12582912]{0:T(1024)(128)(4,1)} %bitcast.183), calls=%async_computation.6 | async-start | bytes 8388608
  283.5 5.4 %slice-start.2 = ((s8[12582912]{0:T(1024)(128)(4,1)}), s8[4194304]{0:T(1024)(128)(4,1)S(1)}, s32[]{:S(2)}) async-start(s8[12582912]{0:T(1024)(128)(4,1)} %bitcast.181), calls=%async_computation.4 | async-start | bytes 8388608
  283.5 6.6 %slice-start.5 = ((s8[12582912]{0:T(1024)(128)(4,1)}), s8[4194304]{0:T(1024)(128)(4,1)S(1)}, s32[]{:S(2)}) async-start(s8[12582912]{0:T(1024)(128)(4,1)} %bitcast.183), calls=%async_computation.7 | async-start | bytes 8388608
  352.8 5.7 %collective-permute-start.5 = (f32[2,64,3,64]{3,1,2,0:T(8,128)S(1)}, f32[2,64,3,64]{3,1,2,0:T(8,128)S(1)}, u32[]{:S(2)}, u32[]{:S(2)}) collective-permute-start(f32[2,64,3,64]{3,1,2,0:T(8,128)S(1)} %get-tuple-element.17), channel_id=1, source_target_pairs={{0,1},{1,0},{2,3},{3,2},{4,5},{5,4},{6,7},{7,6},{8,9},{9,8},{10,11... | collective-permute-start | bytes 294920 | tf_op jit(solution)/shard_map/ppermute | solution.py:12
Sparse Core Ops, SparseCore 0:
  14.1 242.9 all-gather.6
  258.6 44.6 all-gather.4
